TPU v7x, 256 devices: a whole 4x4x8 slice. The times are simulated.
256 devices in a mesh: grp: 8 (over y, z_hi), ep: 32 (over x, z_lo, core).
Axes of the slice: x: 4, y: 4, z: 8 (z_hi: 2, z_lo: 4; z = z_hi * 4 + z_lo), core: 2. Of those that a mesh axis runs over, the one named last changes fastest.
Arguments:
- tokens: bfloat16 [4096, 5120], P('ep', 'grp'), may hold values from -6 to 6
- out_grad: bfloat16 [4096, 5120], P('ep', 'grp'), may hold values from -1.5 to 1.5
- expert_ids: int32 [4096, 6], P('ep'), may hold values from 0 to 23, all different within a row; in each aligned block of 128 rows (0 to 127, 128 to 255, ...) at most 40 rows name the same one
- route_probs: bfloat16 [4096, 6], P('ep'), may hold values from 0.049804688 to 0.59765625
- slot_expert: int32 [32], replicated, may hold values from 0 to 23, as said below
- w_gate: bfloat16 [32, 5120, 1024], P('ep', 'grp'), as said below
- w_up: bfloat16 [32, 5120, 1024], P('ep', 'grp'), as said below
- w_down: bfloat16 [32, 5120, 1024], P('ep', 'grp'), as said below
Outputs:
- in_grad: bfloat16 [4096, 5120], P('ep', 'grp')
- grad_gate: bfloat16 [32, 5120, 1024], P('ep', 'grp')
- grad_up: bfloat16 [32, 5120, 1024], P('ep', 'grp')
- grad_down: bfloat16 [32, 5120, 1024], P('ep', 'grp')
Inputs may be any that keep to these rules, and one draw needn't show every extreme that they name: `expert_ids`: in the rows of one index of ep, no expert is named by more than 40 tokens; some expert is named by exactly 40 in some block. `slot_expert`: every expert 0 to 23 is held by at least one of the 32 slots. `w_gate`: slots that hold the same expert hold equal weights. `w_up`: slots that hold the same expert hold equal weights. `w_down`: slots that hold the same expert hold equal weights.
All inputs are finite; a program needn't handle non-finite values.
Results may differ from a plain program's by a relative error of at most 0.03.
Values may be sent and summed in bfloat16 or wider, within the bound.
No kernel may reach another device: no remote copies, remote signals or barrier semaphores. Data moves between devices by JAX's collectives and lax.ppermute only.
A program may use at most 128 MiB of HBM per device.

v0:
```python
import jax
import jax.numpy as jnp
from jax import lax
from jax.sharding import Mesh, PartitionSpec as P

EP = ("x", "zl", "c")
GRP = ("y", "zh")
BF = jnp.bfloat16
F32 = jnp.float32
CAP = 40


def dot(a, b, dims=((1,), (0,))):
    return lax.dot_general(a, b, (dims, ((), ())), preferred_element_type=F32)


def activate(gate, up_sum, grad_hidden):
    sigma = jax.nn.sigmoid(gate)
    swish = gate * sigma
    hidden = (swish * up_sum).astype(BF)
    grad_up = (grad_hidden * swish).astype(BF)
    grad_gate = (grad_hidden * up_sum * sigma * (1.0 + gate * (1.0 - sigma))).astype(BF)
    return (hidden, grad_gate, grad_up)


def positions(ids, slots_of):
    count = ids.shape[-2]
    sent = jnp.any(ids[..., None] == slots_of, axis=-2)
    row = lax.broadcasted_iota(jnp.int32, (count, count), 0)
    col = lax.broadcasted_iota(jnp.int32, (count, count), 1)
    below = (row > col).astype(BF)
    pos = jnp.einsum("ut,...ts->...us", below, sent.astype(BF), preferred_element_type=F32)
    return jnp.where(sent, pos.astype(jnp.int32), -1)


def turn(value, step):
    return lax.ppermute(value, "y", [(i, (i + step) % 4) for i in range(4)])


def cross(value):
    return lax.ppermute(value, "zh", [(0, 1), (1, 0)])


def rows_at(value, start, size):
    return lax.dynamic_slice_in_dim(value, start, size, 0)


def after(value, *others):
    return lax.optimization_barrier((value, *others))[0]


def send_y(part):
    y = lax.axis_index("y")
    block = part.shape[0] // 4
    got = [turn(rows_at(part, (y + j) % 4 * block, block), j) for j in (1, 3, 2)]
    return [rows_at(part, y * block, block)] + got


def sum_y(part):
    return [lax.psum_scatter(part, "y", scatter_dimension=0, tiled=True)]


def add_up(pieces):
    total = pieces[0].astype(F32)
    for g in pieces[1:]:
        total = total + g.astype(F32)
    return total


def spread_y(mine):
    half = mine.shape[0] // 2
    left, right = turn(mine, 1), turn(mine, -1)
    far0, far1 = turn(left[:half], 1), turn(right[half:], -1)
    return [mine, left, right, far0, far1]


def lay(pieces):
    y = lax.axis_index("y")
    block, cols = pieces[0].shape
    out = jnp.zeros((4 * block, cols), BF)
    for piece, j, lo in zip(pieces, (0, 3, 1, 2, 2), (0, 0, 0, 0, block // 2)):
        out = lax.dynamic_update_slice(out, piece, ((y + j) % 4 * block + lo, 0))
    return out


SIZES = (24, 16)
WIDE = ("x", "c", "zl")


def per_device(tokens, out_grad, expert_ids, route_probs, slot_expert, w_gate, w_up, w_down):
    count, width = tokens.shape
    slots = slot_expert.shape[0]
    wd = w_down[0]
    wgu = jnp.concatenate([w_gate[0], w_up[0]], axis=1)
    mid = wd.shape[1]
    size0, size1 = SIZES
    mixed = slot_expert.reshape(4, 4, 2).transpose(0, 2, 1).reshape(slots)

    pos = positions(expert_ids, mixed).T

    def picked(where, lo, size):
        place = lax.broadcasted_iota(jnp.int32, (slots, size, count), 1) + lo
        return (where[:, None, :] == place).astype(BF).reshape(slots * size, count)

    def move(value, axes):
        return lax.all_to_all(value, axes, 0, 0, tiled=True)

    def send_x(lo, size):
        return dot(picked(pos, lo, size), tokens).astype(BF).reshape(slots, size, width)

    xs0 = move(send_x(0, size0), WIDE)

    weight = jnp.sum(jnp.where(expert_ids[:, :, None] == mixed, route_probs.astype(F32)[:, :, None], 0.0), axis=1).T

    def send_g(lo, size):
        place = lax.broadcasted_iota(jnp.int32, (slots, size, count), 1) + lo
        matrix = jnp.where(pos[:, None, :] == place, weight[:, None, :], 0.0).astype(BF)
        return dot(matrix.reshape(slots * size, count), out_grad).astype(BF).reshape(slots, size, width)

    gs0 = move(after(send_g(0, size0), xs0), WIDE)
    both1 = jnp.concatenate([send_x(size0, size1), send_g(size0, size1)], axis=2)
    both1 = move(after(both1, gs0), WIDE).reshape(slots * size1, 2 * width)
    xs0, gs0 = xs0.reshape(slots * size0, width), gs0.reshape(slots * size0, width)
    xs1, gs1 = both1[:, :width], both1[:, width:]

    def act(gu, dh):
        hidden, d_gate, d_up = activate(gu[:, :mid], gu[:, mid:], dh)
        return jnp.concatenate([d_gate, d_up, hidden], axis=1)

    gu0 = sum_y(dot(xs0, wgu).astype(BF))
    dh0 = send_y(dot(gs0, wd).astype(BF))
    gu0_sum = add_up(gu0)
    gu0_got = cross(gu0_sum.astype(BF))
    dh0_sum = add_up(dh0)
    dh0_got = cross(dh0_sum.astype(BF))
    part1 = jnp.concatenate([dot(xs1, wgu).astype(BF), dot(gs1, wd).astype(BF)], axis=1)
    part1 = after(part1, *dh0)
    all1 = send_y(part1)
    own0 = act(gu0_sum + gu0_got.astype(F32), dh0_sum + dh0_got.astype(F32))
    all1[0] = after(all1[0], gu0_got, dh0_got)
    own0 = after(own0, *all1)
    all1_sum = add_up(all1)
    all1_got = cross(all1_sum.astype(BF))
    got0 = spread_y(own0)
    all1_got = after(all1_got, got0[1], got0[2])
    all1_sum = all1_sum + all1_got.astype(F32)
    own1 = act(all1_sum[:, : 2 * mid], all1_sum[:, 2 * mid :])
    own1 = after(own1, got0[3], got0[4])
    got1 = spread_y(own1)

    slot = jnp.arange(slots)
    same = (mixed[:, None] == mixed[None, :]) & (slot[:, None] > slot[None, :])
    first = jnp.logical_not(jnp.any(same, axis=1))
    where_to = jnp.where(first[:, None], pos, -1)

    def back(ret, lo, size):
        return dot(picked(where_to, lo, size), ret.reshape(slots * size, width), ((0,), (0,)))

    def row_grad(full, size):
        rg = dot(full[:, : 2 * mid], wgu, ((1,), (1,))).astype(BF)
        return move(rg.reshape(slots, size, width), WIDE)

    def weight_grad(full, xs, gs):
        return [
            dot(xs, full[:, :mid], ((0,), (0,))),
            dot(xs, full[:, mid : 2 * mid], ((0,), (0,))),
            dot(gs, full[:, 2 * mid :], ((0,), (0,))),
        ]

    full0 = lay(got0)
    ret0 = row_grad(full0, size0)
    full0 = after(full0, got1[1], got1[2])
    parts0 = weight_grad(full0, xs0, gs0)
    got1[3] = after(got1[3], *parts0)
    full1 = lay(got1)
    ret1 = row_grad(full1, size1)
    parts1 = weight_grad(full1, xs1, gs1)
    in_grad = (back(ret0, 0, size0) + back(ret1, size0, size1)).astype(BF)
    pg, pu, pd = [(p + q).astype(BF) for p, q in zip(parts0, parts1)]
    return in_grad, pg[None], pu[None], pd[None]


def solution(mesh):
    fine = Mesh(mesh.devices.reshape(4, 2, 4, 4, 2), ("y", "zh", "x", "zl", "c"))
    return jax.shard_map(
        per_device,
        mesh=fine,
        in_specs=(
            P(EP, GRP),
            P(EP, GRP),
            P(EP, None),
            P(EP, None),
            P(),
            P(EP, GRP, None),
            P(EP, GRP, None),
            P(EP, GRP, None),
        ),
        out_specs=(P(EP, GRP), P(EP, GRP, None), P(EP, GRP, None), P(EP, GRP, None)),
        check_vma=False,
    )
```

profile of v0, /device:TPU:1, one launch (start us, length us, event | category | flops | bytes accessed | tf_op | source)
XLA Modules:
  0.0 297.7 jit_solution(17451724554012960921)
XLA Ops:
  11.1 35.1 %all_to_all.25 = bf16[32,24,640]{2,1,0:T(8,128)(2,1)S(1)} all-to-all(bf16[32,24,640]{2,1,0:T(8,128)(2,1)S(1)} %bitcast.69), channel_id=1, replica_groups=mesh['y'=4,'zh'=2,'x'=4,'zl'=4,'c'=2] {'x','c','zl'}, dimensions={0} | all-to-all | bytes 1966080 | tf_op jit(solution)/shard_map/all_to_all | solution.py:106
  47.2 4.1 %convolution_convert_fusion = bf16[768,2048]{1,0:T(8,128)(2,1)} fusion(bf16[768,640]{1,0:T(8,128)(2,1)S(1)} %bitcast.72, bf16[640,1024]{1,0:T(8,128)(2,1)S(1)} %bitcast.79, bf16[640,1024]{1,0:T(8,128)(2,1)S(1)} %bitcast.83), kind=kOutput, calls=%fused_computation | convolution fusion | flops 2020081664 | bytes 6750208 | tf_op jit(solution)/shard_map/dot_general | solution.py:14
  53.7 5.5 %all-to-all-start.1 = ((bf16[32,24,640]{2,1,0:T(8,128)(2,1)}), bf16[32,24,640]{2,1,0:T(8,128)(2,1)}, u32[]{:S(2)}, u32[]{:S(2)}) async-start(bf16[32,24,640]{2,1,0:T(8,128)(2,1)} %bitcast.5), calls=%async_computation.1 | async-start | bytes 1966080 | tf_op jit(solution)/shard_map/all_to_all | solution.py:106
  61.4 23.1 %all-to-all-done.1 = bf16[32,24,640]{2,1,0:T(8,128)(2,1)} async-done(((bf16[32,24,640]{2,1,0:T(8,128)(2,1)}), bf16[32,24,640]{2,1,0:T(8,128)(2,1)}, u32[]{:S(2)}, u32[]{:S(2)}) %all-to-all-start.1) | async-done | bytes 983072 | tf_op jit(solution)/shard_map/all_to_all | solution.py:106
  84.5 5.4 %all-to-all-start.2 = ((bf16[32,16,1280]{2,1,0:T(8,128)(2,1)}), bf16[32,16,1280]{2,1,0:T(8,128)(2,1)S(1)}, u32[]{:S(2)}, u32[]{:S(2)}) async-start(bf16[32,16,1280]{2,1,0:T(8,128)(2,1)} %pad_maximum_fusion.2), calls=%async_computation.3 | async-start | bytes 2621440 | tf_op jit(solution)/shard_map/all_to_all | solution.py:106
  98.1 7.9 %collective-permute-done.2 = bf16[192,1024]{1,0:T(8,128)(2,1)S(1)} collective-permute-done((bf16[192,1024]{1,0:T(8,128)(2,1)}, bf16[192,1024]{1,0:T(8,128)(2,1)S(1)}, u32[]{:S(2)}, u32[]{:S(2)}) %collective-permute-start.2) | collective-permute-done | bytes 393248 | tf_op jit(solution)/shard_map/ppermute | solution.py:37
  106.0 8.9 %collective-permute-done.1 = bf16[192,1024]{1,0:T(8,128)(2,1)S(1)} collective-permute-done((bf16[192,1024]{1,0:T(8,128)(2,1)}, bf16[192,1024]{1,0:T(8,128)(2,1)S(1)}, u32[]{:S(2)}, u32[]{:S(2)}) %collective-permute-start.1) | collective-permute-done | bytes 393248 | tf_op jit(solution)/shard_map/ppermute | solution.py:37
  117.3 4.2 %collective-permute-start.3 = (bf16[192,1024]{1,0:T(8,128)(2,1)}, bf16[192,1024]{1,0:T(8,128)(2,1)}, u32[]{:S(2)}, u32[]{:S(2)}) collective-permute-start(bf16[192,1024]{1,0:T(8,128)(2,1)} %get-tuple-element.22), channel_id=1, source_target_pairs={{0,32},{32,0},{1,33},{33,1},{2,34},{34,2},{3,35},{35,3},{4,36},{36... | collective-permute-start | bytes 1179656 | tf_op jit(solution)/shard_map/ppermute | solution.py:41
  123.8 3.2 %convolution_convert_fusion.1 = bf16[512,2048]{1,0:T(8,128)(2,1)} fusion(bf16[512,1280]{1,0:T(8,128)(2,1)S(1)} %bitcast.65, bf16[640,1024]{1,0:T(8,128)(2,1)S(1)} %bitcast.80, bf16[640,1024]{1,0:T(8,128)(2,1)S(1)} %bitcast.84), kind=kOutput, calls=%fused_computation.4 | convolution fusion | flops 1348468736 | bytes 5373952 | tf_op jit(solution)/shard_map/dot_general | solution.py:14
  126.9 4.2 %collective-permute-start.4 = (bf16[192,2048]{1,0:T(8,128)(2,1)}, bf16[192,2048]{1,0:T(8,128)(2,1)S(1)}, u32[]{:S(2)}, u32[]{:S(2)}) collective-permute-start(bf16[192,2048]{1,0:T(8,128)(2,1)} %reduce-scatter.2.cloned.1.call-done), channel_id=1, source_target_pairs={{0,32},{32,0},{1,33},{33,1},{2,34},{34,2},{3,35},{35,3},{4,36},{36... | collective-permute-start | bytes 2359304 | tf_op jit(solution)/shard_map/ppermute | solution.py:41
  137.9 17.5 %collective-permute-done.4 = bf16[192,2048]{1,0:T(8,128)(2,1)S(1)} collective-permute-done((bf16[192,2048]{1,0:T(8,128)(2,1)}, bf16[192,2048]{1,0:T(8,128)(2,1)S(1)}, u32[]{:S(2)}, u32[]{:S(2)}) %collective-permute-start.4) | collective-permute-done | bytes 786464 | tf_op jit(solution)/shard_map/ppermute | solution.py:41
  158.5 13.2 %collective-permute-done.7 = bf16[128,3072]{1,0:T(8,128)(2,1)S(1)} collective-permute-done((bf16[128,3072]{1,0:T(8,128)(2,1)S(1)}, bf16[128,3072]{1,0:T(8,128)(2,1)S(1)}, u32[]{:S(2)}, u32[]{:S(2)}) %collective-permute-start.7) | collective-permute-done | bytes 786464 | tf_op jit(solution)/shard_map/ppermute | solution.py:37
  178.3 22.0 %collective-permute-done.8 = bf16[192,3072]{1,0:T(8,128)(2,1)} collective-permute-done((bf16[192,3072]{1,0:T(8,128)(2,1)}, bf16[192,3072]{1,0:T(8,128)(2,1)}, u32[]{:S(2)}, u32[]{:S(2)}) %collective-permute-start.8) | collective-permute-done | bytes 1179680 | tf_op jit(solution)/shard_map/ppermute | solution.py:37
  210.5 5.8 %collective-permute-done.10 = bf16[96,3072]{1,0:T(8,128)(2,1)S(1)} collective-permute-done((bf16[96,3072]{1,0:T(8,128)(2,1)S(1)}, bf16[96,3072]{1,0:T(8,128)(2,1)S(1)}, u32[]{:S(2)}, u32[]{:S(2)}) %collective-permute-start.10) | collective-permute-done | bytes 589856 | tf_op jit(solution)/shard_map/ppermute | solution.py:37
  216.8 3.1 %collective-permute-start.14 = (bf16[128,3072]{1,0:T(8,128)(2,1)S(1)}, bf16[128,3072]{1,0:T(8,128)(2,1)}, u32[]{:S(2)}, u32[]{:S(2)}) collective-permute-start(bf16[128,3072]{1,0:T(8,128)(2,1)S(1)} %pad_maximum_fusion.4), channel_id=1, source_target_pairs={{0,192},{64,0},{128,64},{192,128},{1,193},{65,1},{129,65},{193,129... | collective-permute-start | bytes 2359304 | tf_op jit(solution)/shard_map/ppermute | solution.py:37
  220.1 3.6 %fusion.10 = bf16[768,640]{1,0:T(8,128)(2,1)} fusion(bf16[768,3072]{1,0:T(8,128)(2,1)S(1)} %constant_dynamic-update-slice_fusion.5, bf16[640,1024]{1,0:T(8,128)(2,1)S(1)} %bitcast.81, bf16[640,1024]{1,0:T(8,128)(2,1)S(1)} %bitcast.85), kind=kOutput, calls=%fused_computation.24 | convolution fusion | flops 2019000320 | bytes 6750208 | tf_op jit(solution)/shard_map/dot_general | solution.py:14
  223.7 15.5 %all-to-all-start.3 = ((bf16[32,24,640]{2,1,0:T(8,128)(2,1)}), bf16[32,24,640]{2,1,0:T(8,128)(2,1)}, u32[]{:S(2)}, u32[]{:S(2)}) async-start(bf16[32,24,640]{2,1,0:T(8,128)(2,1)} %bitcast.75), calls=%async_computation.4 | async-start | bytes 1966080 | tf_op jit(solution)/shard_map/all_to_all | solution.py:106
  241.0 3.1 %collective-permute-start.16 = (bf16[64,3072]{1,0:T(8,128)(2,1)S(1)}, bf16[64,3072]{1,0:T(8,128)(2,1)S(1)}, u32[]{:S(2)}, u32[]{:S(2)}) collective-permute-start(bf16[64,3072]{1,0:T(8,128)(2,1)S(1)} %slice.90), channel_id=1, source_target_pairs={{0,192},{64,0},{128,64},{192,128},{1,193},{65,1},{129,65},{193,129... | collective-permute-start | bytes 1179656 | tf_op jit(solution)/shard_map/ppermute | solution.py:37
  250.8 4.1 %fusion.4 = f32[640,1024]{1,0:T(8,128)} fusion(bf16[768,640]{1,0:T(8,128)(2,1)} %bitcast.7, bf16[768,3072]{1,0:T(8,128)(2,1)S(1)} %copy-done.5), kind=kOutput, calls=%fused_computation.12 | convolution fusion | flops 1006632960 | bytes 5177344 | tf_op jit(solution)/shard_map/dot_general | solution.py:14
  259.3 5.2 %all-to-all-done.3 = bf16[32,24,640]{2,1,0:T(8,128)(2,1)} async-done(((bf16[32,24,640]{2,1,0:T(8,128)(2,1)}), bf16[32,24,640]{2,1,0:T(8,128)(2,1)}, u32[]{:S(2)}, u32[]{:S(2)}) %all-to-all-start.3) | async-done | bytes 983072 | tf_op jit(solution)/shard_map/all_to_all | solution.py:106
  264.5 6.3 %all-to-all-start.4 = ((bf16[32,16,640]{2,1,0:T(8,128)(2,1)}), bf16[32,16,640]{2,1,0:T(8,128)(2,1)S(1)}, u32[]{:S(2)}, u32[]{:S(2)}) async-start(bf16[32,16,640]{2,1,0:T(8,128)(2,1)} %bitcast.19), calls=%async_computation.5 | async-start | bytes 1310720 | tf_op jit(solution)/shard_map/all_to_all | solution.py:106
  270.9 4.1 %fusion.13 = bf16[1,640,1024]{2,1,0:T(8,128)(2,1)} fusion(f32[640,1024]{1,0:T(8,128)} %fusion.8, bf16[512,3072]{1,0:T(8,128)(2,1)} %copy-done.2, bf16[512,1280]{1,0:T(8,128)(2,1)S(1)} %bitcast.66), kind=kOutput, calls=%fused_computation.25 | convolution fusion | flops 672399360 | bytes 5636096 | tf_op jit(solution)/shard_map/dot_general | solution.py:14
  275.0 3.8 %fusion.14 = bf16[1,640,1024]{2,1,0:T(8,128)(2,1)} fusion(f32[640,1024]{1,0:T(8,128)} %fusion.6, bf16[512,3072]{1,0:T(8,128)(2,1)S(1)} %copy-done.3, bf16[512,1280]{1,0:T(8,128)(2,1)S(1)} %bitcast.67), kind=kOutput, calls=%fused_computation.26 | convolution fusion | flops 672399360 | bytes 5636096 | tf_op jit(solution)/shard_map/dot_general | solution.py:14
  282.4 7.4 %all-to-all-done.4 = bf16[32,16,640]{2,1,0:T(8,128)(2,1)S(1)} async-done(((bf16[32,16,640]{2,1,0:T(8,128)(2,1)}), bf16[32,16,640]{2,1,0:T(8,128)(2,1)S(1)}, u32[]{:S(2)}, u32[]{:S(2)}) %all-to-all-start.4) | async-done | bytes 655392 | tf_op jit(solution)/shard_map/all_to_all | solution.py:106
  (152 shorter events, 66.6 us)
Async XLA Ops:
  7.2 82.8 %copy-start = (bf16[1,640,1024]{2,1,0:T(8,128)(2,1)S(1)}, bf16[1,640,1024]{2,1,0:T(8,128)(2,1)}, u32[]{:S(2)}) copy-start(bf16[1,640,1024]{2,1,0:T(8,128)(2,1)} %param.15) | copy-start | bytes 3932164
  7.2 119.8 %reduce-scatter.2.cloned.1.call-start = ((), (), s32[]{:S(2)}) async-start(), calls=%async_computation.6 | async-start | bytes 3932160 | tf_op jit(solution)/shard_map/reduce_scatter | solution.py:60
  8.3 38.9 %copy-start.29 = (bf16[1,640,1024]{2,1,0:T(8,128)(2,1)S(1)}, bf16[1,640,1024]{2,1,0:T(8,128)(2,1)}, u32[]{:S(2)}) copy-start(bf16[1,640,1024]{2,1,0:T(8,128)(2,1)} %param.13) | copy-start | bytes 3932164
  53.7 30.8 %all-to-all-start.1 = ((bf16[32,24,640]{2,1,0:T(8,128)(2,1)}), bf16[32,24,640]{2,1,0:T(8,128)(2,1)}, u32[]{:S(2)}, u32[]{:S(2)}) async-start(bf16[32,24,640]{2,1,0:T(8,128)(2,1)} %bitcast.5), calls=%async_computation.1 | async-start | bytes 1966080 | tf_op jit(solution)/shard_map/all_to_all | solution.py:106
  84.5 37.3 %all-to-all-start.2 = ((bf16[32,16,1280]{2,1,0:T(8,128)(2,1)}), bf16[32,16,1280]{2,1,0:T(8,128)(2,1)S(1)}, u32[]{:S(2)}, u32[]{:S(2)}) async-start(bf16[32,16,1280]{2,1,0:T(8,128)(2,1)} %pad_maximum_fusion.2), calls=%async_computation.3 | async-start | bytes 2621440 | tf_op jit(solution)/shard_map/all_to_all | solution.py:106
  93.7 12.2 %collective-permute-start.2 = (bf16[192,1024]{1,0:T(8,128)(2,1)}, bf16[192,1024]{1,0:T(8,128)(2,1)S(1)}, u32[]{:S(2)}, u32[]{:S(2)}) collective-permute-start(bf16[192,1024]{1,0:T(8,128)(2,1)} %get-tuple-element.35), channel_id=1, source_target_pairs={{0,128},{64,192},{128,0},{192,64},{1,129},{65,193},{129,1},{193,65... | collective-permute-start | bytes 1179656 | tf_op jit(solution)/shard_map/ppermute | solution.py:37
  96.7 18.2 %collective-permute-start.1 = (bf16[192,1024]{1,0:T(8,128)(2,1)}, bf16[192,1024]{1,0:T(8,128)(2,1)S(1)}, u32[]{:S(2)}, u32[]{:S(2)}) collective-permute-start(bf16[192,1024]{1,0:T(8,128)(2,1)} %get-tuple-element.36), channel_id=1, source_target_pairs={{0,192},{64,0},{128,64},{192,128},{1,193},{65,1},{129,65},{193,129... | collective-permute-start | bytes 1179656 | tf_op jit(solution)/shard_map/ppermute | solution.py:37
  97.4 17.6 %collective-permute-start = (bf16[192,1024]{1,0:T(8,128)(2,1)}, bf16[192,1024]{1,0:T(8,128)(2,1)}, u32[]{:S(2)}, u32[]{:S(2)}) collective-permute-start(bf16[192,1024]{1,0:T(8,128)(2,1)} %get-tuple-element.34), channel_id=1, source_target_pairs={{0,64},{64,128},{128,192},{192,0},{1,65},{65,129},{129,193},{193,1... | collective-permute-start | bytes 1179656 | tf_op jit(solution)/shard_map/ppermute | solution.py:37
  117.3 38.2 %collective-permute-start.3 = (bf16[192,1024]{1,0:T(8,128)(2,1)}, bf16[192,1024]{1,0:T(8,128)(2,1)}, u32[]{:S(2)}, u32[]{:S(2)}) collective-permute-start(bf16[192,1024]{1,0:T(8,128)(2,1)} %get-tuple-element.22), channel_id=1, source_target_pairs={{0,32},{32,0},{1,33},{33,1},{2,34},{34,2},{3,35},{35,3},{4,36},{36... | collective-permute-start | bytes 1179656 | tf_op jit(solution)/shard_map/ppermute | solution.py:41
  126.9 28.4 %collective-permute-start.4 = (bf16[192,2048]{1,0:T(8,128)(2,1)}, bf16[192,2048]{1,0:T(8,128)(2,1)S(1)}, u32[]{:S(2)}, u32[]{:S(2)}) collective-permute-start(bf16[192,2048]{1,0:T(8,128)(2,1)} %reduce-scatter.2.cloned.1.call-done), channel_id=1, source_target_pairs={{0,32},{32,0},{1,33},{33,1},{2,34},{34,2},{3,35},{35,3},{4,36},{36... | collective-permute-start | bytes 2359304 | tf_op jit(solution)/shard_map/ppermute | solution.py:41
  133.2 25.3 %collective-permute-start.5 = (bf16[128,3072]{1,0:T(8,128)(2,1)S(1)}, bf16[128,3072]{1,0:T(8,128)(2,1)S(1)}, u32[]{:S(2)}, u32[]{:S(2)}) collective-permute-start(bf16[128,3072]{1,0:T(8,128)(2,1)S(1)} %get-tuple-element.28), channel_id=1, source_target_pairs={{0,64},{64,128},{128,192},{192,0},{1,65},{65,129},{129,193},{193,1... | collective-permute-start | bytes 2359304 | tf_op jit(solution)/shard_map/ppermute | solution.py:37
  134.8 23.7 %collective-permute-start.6 = (bf16[128,3072]{1,0:T(8,128)(2,1)S(1)}, bf16[128,3072]{1,0:T(8,128)(2,1)S(1)}, u32[]{:S(2)}, u32[]{:S(2)}) collective-permute-start(bf16[128,3072]{1,0:T(8,128)(2,1)S(1)} %get-tuple-element.27), channel_id=1, source_target_pairs={{0,192},{64,0},{128,64},{192,128},{1,193},{65,1},{129,65},{193,129... | collective-permute-start | bytes 2359304 | tf_op jit(solution)/shard_map/ppermute | solution.py:37
  136.3 35.4 %collective-permute-start.7 = (bf16[128,3072]{1,0:T(8,128)(2,1)S(1)}, bf16[128,3072]{1,0:T(8,128)(2,1)S(1)}, u32[]{:S(2)}, u32[]{:S(2)}) collective-permute-start(bf16[128,3072]{1,0:T(8,128)(2,1)S(1)} %get-tuple-element.26), channel_id=1, source_target_pairs={{0,128},{64,192},{128,0},{192,64},{1,129},{65,193},{129,1},{193,65... | collective-permute-start | bytes 2359304 | tf_op jit(solution)/shard_map/ppermute | solution.py:37
  171.7 28.7 %collective-permute-start.8 = (bf16[192,3072]{1,0:T(8,128)(2,1)}, bf16[192,3072]{1,0:T(8,128)(2,1)}, u32[]{:S(2)}, u32[]{:S(2)}) collective-permute-start(bf16[192,3072]{1,0:T(8,128)(2,1)} %pad_maximum_fusion.3), channel_id=1, source_target_pairs={{0,64},{64,128},{128,192},{192,0},{1,65},{65,129},{129,193},{193,1... | collective-permute-start | bytes 3538952 | tf_op jit(solution)/shard_map/ppermute | solution.py:37
  173.0 28.7 %collective-permute-start.9 = (bf16[192,3072]{1,0:T(8,128)(2,1)}, bf16[192,3072]{1,0:T(8,128)(2,1)}, u32[]{:S(2)}, u32[]{:S(2)}) collective-permute-start(bf16[192,3072]{1,0:T(8,128)(2,1)} %pad_maximum_fusion.3), channel_id=1, source_target_pairs={{0,192},{64,0},{128,64},{192,128},{1,193},{65,1},{129,65},{193,129... | collective-permute-start | bytes 3538952 | tf_op jit(solution)/shard_map/ppermute | solution.py:37
  175.7 29.7 %collective-permute-start.12 = (bf16[128,3072]{1,0:T(8,128)(2,1)}, bf16[128,3072]{1,0:T(8,128)(2,1)}, u32[]{:S(2)}, u32[]{:S(2)}) collective-permute-start(bf16[128,3072]{1,0:T(8,128)(2,1)} %fusion.33), channel_id=1, source_target_pairs={{0,32},{32,0},{1,33},{33,1},{2,34},{34,2},{3,35},{35,3},{4,36},{36... | collective-permute-start | bytes 2359304 | tf_op jit(solution)/shard_map/ppermute | solution.py:41
  201.5 14.9 %collective-permute-start.10 = (bf16[96,3072]{1,0:T(8,128)(2,1)S(1)}, bf16[96,3072]{1,0:T(8,128)(2,1)S(1)}, u32[]{:S(2)}, u32[]{:S(2)}) collective-permute-start(bf16[96,3072]{1,0:T(8,128)(2,1)S(1)} %slice.83), channel_id=1, source_target_pairs={{0,64},{64,128},{128,192},{192,0},{1,65},{65,129},{129,193},{193,1... | collective-permute-start | bytes 1769480 | tf_op jit(solution)/shard_map/ppermute | solution.py:37
  202.8 13.8 %collective-permute-start.11 = (bf16[96,3072]{1,0:T(8,128)(2,1)S(1)}, bf16[96,3072]{1,0:T(8,128)(2,1)S(1)}, u32[]{:S(2)}, u32[]{:S(2)}) collective-permute-start(bf16[96,3072]{1,0:T(8,128)(2,1)S(1)} %slice.84), channel_id=1, source_target_pairs={{0,192},{64,0},{128,64},{192,128},{1,193},{65,1},{129,65},{193,129... | collective-permute-start | bytes 1769480 | tf_op jit(solution)/shard_map/ppermute | solution.py:37
  216.5 23.1 %collective-permute-start.13 = (bf16[128,3072]{1,0:T(8,128)(2,1)S(1)}, bf16[128,3072]{1,0:T(8,128)(2,1)S(1)}, u32[]{:S(2)}, u32[]{:S(2)}) collective-permute-start(bf16[128,3072]{1,0:T(8,128)(2,1)S(1)} %pad_maximum_fusion.4), channel_id=1, source_target_pairs={{0,64},{64,128},{128,192},{192,0},{1,65},{65,129},{129,193},{193,1... | collective-permute-start | bytes 2359304 | tf_op jit(solution)/shard_map/ppermute | solution.py:37
  216.8 23.0 %collective-permute-start.14 = (bf16[128,3072]{1,0:T(8,128)(2,1)S(1)}, bf16[128,3072]{1,0:T(8,128)(2,1)}, u32[]{:S(2)}, u32[]{:S(2)}) collective-permute-start(bf16[128,3072]{1,0:T(8,128)(2,1)S(1)} %pad_maximum_fusion.4), channel_id=1, source_target_pairs={{0,192},{64,0},{128,64},{192,128},{1,193},{65,1},{129,65},{193,129... | collective-permute-start | bytes 2359304 | tf_op jit(solution)/shard_map/ppermute | solution.py:37
  223.7 40.9 %all-to-all-start.3 = ((bf16[32,24,640]{2,1,0:T(8,128)(2,1)}), bf16[32,24,640]{2,1,0:T(8,128)(2,1)}, u32[]{:S(2)}, u32[]{:S(2)}) async-start(bf16[32,24,640]{2,1,0:T(8,128)(2,1)} %bitcast.75), calls=%async_computation.4 | async-start | bytes 1966080 | tf_op jit(solution)/shard_map/all_to_all | solution.py:106
  239.7 15.2 %collective-permute-start.15 = (bf16[64,3072]{1,0:T(8,128)(2,1)S(1)}, bf16[64,3072]{1,0:T(8,128)(2,1)S(1)}, u32[]{:S(2)}, u32[]{:S(2)}) collective-permute-start(bf16[64,3072]{1,0:T(8,128)(2,1)S(1)} %slice.89), channel_id=1, source_target_pairs={{0,64},{64,128},{128,192},{192,0},{1,65},{65,129},{129,193},{193,1... | collective-permute-start | bytes 1179656 | tf_op jit(solution)/shard_map/ppermute | solution.py:37
  241.0 13.9 %collective-permute-start.16 = (bf16[64,3072]{1,0:T(8,128)(2,1)S(1)}, bf16[64,3072]{1,0:T(8,128)(2,1)S(1)}, u32[]{:S(2)}, u32[]{:S(2)}) collective-permute-start(bf16[64,3072]{1,0:T(8,128)(2,1)S(1)} %slice.90), channel_id=1, source_target_pairs={{0,192},{64,0},{128,64},{192,128},{1,193},{65,1},{129,65},{193,129... | collective-permute-start | bytes 1179656 | tf_op jit(solution)/shard_map/ppermute | solution.py:37
  264.5 25.3 %all-to-all-start.4 = ((bf16[32,16,640]{2,1,0:T(8,128)(2,1)}), bf16[32,16,640]{2,1,0:T(8,128)(2,1)S(1)}, u32[]{:S(2)}, u32[]{:S(2)}) async-start(bf16[32,16,640]{2,1,0:T(8,128)(2,1)} %bitcast.19), calls=%async_computation.5 | async-start | bytes 1310720 | tf_op jit(solution)/shard_map/all_to_all | solution.py:106
  (31 other events, 329.0 us)
Sparse Core Ops, SparseCore 0:
  51.5 39.9 reduce-scatter.1
where the time goes:
time: 299 us; the launch traced here: 298 us
  waiting for transfers between devices  112 us (37%)
  starting transfers between devices  62.8 us (21%)
  matrix products  43.6 us (15%)
  blocking collectives  35.1 us (12%)
  local copies, waits for them, and re-layouts  16.3 us (5%)
  between operations  14.7 us (5%)
  other arithmetic  13.7 us (5%)
    ppermute x14, waiting for transfers between devices, turn(): return lax.ppermute(value, 'y', [(i, (i + step) % 4) for i in range(4)])  58.1 us
    dot_general x18, matrix products, dot(): return lax.dot_general(a, b, (dims, ((), ())), preferred_element_type=F32)  43.5 us
    all_to_all x4, waiting for transfers between devices, move(): return lax.all_to_all(value, axes, 0, 0, tiled=True)  36 us
    all_to_all x1, blocking collectives, move(): return lax.all_to_all(value, axes, 0, 0, tiled=True)  35.1 us
    all_to_all x4, starting transfers between devices, move(): return lax.all_to_all(value, axes, 0, 0, tiled=True)  32.7 us
    ppermute x14, starting transfers between devices, turn(): return lax.ppermute(value, 'y', [(i, (i + step) % 4) for i in range(4)])  21.1 us
    ppermute x3, waiting for transfers between devices, cross(): return lax.ppermute(value, 'zh', [(0, 1), (1, 0)])  17.5 us
    ppermute x3, starting transfers between devices, cross(): return lax.ppermute(value, 'zh', [(0, 1), (1, 0)])  8.93 us
  transfers between devices with their start and end apart: 22, of which 12 were waited for; matrix products, arithmetic and copies ran while one was open for 21% of the time, Pallas kernels for 0%

commit v1 on v0

--- a/solution.py
+++ b/solution.py
@@ -171,7 +171,7 @@
     ret0 = row_grad(full0, size0)
     full0 = after(full0, got1[1], got1[2])
     parts0 = weight_grad(full0, xs0, gs0)
-    got1[3] = after(got1[3], *parts0)
+    got1[3] = after(got1[3], *parts0[:2])
     full1 = lay(got1)
     ret1 = row_grad(full1, size1)
     parts1 = weight_grad(full1, xs1, gs1)

time: 299 us -> 301 us (level)
  starting transfers between devices: 62.8 us -> 70.2 us
  waiting for transfers between devices: 112 us -> 107 us
  matrix products: 43.6 us -> 39.1 us
    ppermute x14, waiting for transfers between devices: 58.1 us -> 35.8 us  [turn(): return lax.ppermute(value, 'y', [(i, (i + step) % 4) for i in range(4)])]
    ppermute x3, waiting for transfers between devices: 17.5 us -> 33.7 us  [cross(): return lax.ppermute(value, 'zh', [(0, 1), (1, 0)])]
    ppermute x3, starting transfers between devices: 8.93 us -> 17.2 us  [cross(): return lax.ppermute(value, 'zh', [(0, 1), (1, 0)])]
    dot_general x18, matrix products: 43.5 us -> 39 us  [dot(): return lax.dot_general(a, b, (dims, ((), ())), preferred_element_type=F32)]
  transfers between devices with their start and end apart: 22 -> 22, of which waited for: 12 -> 14; matrix products, arithmetic and copies ran while one was open for 21% -> 19% of each run, Pallas kernels for 0% -> 0%
where the time goes in v1:
time: 301 us; the launch traced here: 299 us
  waiting for transfers between devices  107 us (36%)
  starting transfers between devices  70.2 us (23%)
  matrix products  39.1 us (13%)
  blocking collectives  35.1 us (12%)
  local copies, waits for them, and re-layouts  19.1 us (6%)
  between operations  14.7 us (5%)
  other arithmetic  13.6 us (5%)
    dot_general x18, matrix products, dot(): return lax.dot_general(a, b, (dims, ((), ())), preferred_element_type=F32)  39 us
    all_to_all x4, waiting for transfers between devices, move(): return lax.all_to_all(value, axes, 0, 0, tiled=True)  37.9 us
    ppermute x14, waiting for transfers between devices, turn(): return lax.ppermute(value, 'y', [(i, (i + step) % 4) for i in range(4)])  35.8 us
    all_to_all x1, blocking collectives, move(): return lax.all_to_all(value, axes, 0, 0, tiled=True)  35.1 us
    ppermute x3, waiting for transfers between devices, cross(): return lax.ppermute(value, 'zh', [(0, 1), (1, 0)])  33.7 us
    all_to_all x4, starting transfers between devices, move(): return lax.all_to_all(value, axes, 0, 0, tiled=True)  32.4 us
    ppermute x14, starting transfers between devices, turn(): return lax.ppermute(value, 'y', [(i, (i + step) % 4) for i in range(4)])  20.6 us
    ppermute x3, starting transfers between devices, cross(): return lax.ppermute(value, 'zh', [(0, 1), (1, 0)])  17.2 us
  transfers between devices with their start and end apart: 22, of which 14 were waited for; matrix products, arithmetic and copies ran while one was open for 19% of the time, Pallas kernels for 0%

profile of v1, /device:TPU:1, one launch (start us, length us, event | category | flops | bytes accessed | tf_op | source)
XLA Modules:
  0.0 299.4 jit_solution(3182854675866341268)
XLA Ops:
  11.1 35.1 %all_to_all.25 = bf16[32,24,640]{2,1,0:T(8,128)(2,1)S(1)} all-to-all(bf16[32,24,640]{2,1,0:T(8,128)(2,1)S(1)} %bitcast.69), channel_id=1, replica_groups=mesh['y'=4,'zh'=2,'x'=4,'zl'=4,'c'=2] {'x','c','zl'}, dimensions={0} | all-to-all | bytes 1966080 | tf_op jit(solution)/shard_map/all_to_all | solution.py:106
  47.2 4.1 %convolution_convert_fusion = bf16[768,2048]{1,0:T(8,128)(2,1)} fusion(bf16[768,640]{1,0:T(8,128)(2,1)S(1)} %bitcast.74, bf16[640,1024]{1,0:T(8,128)(2,1)S(1)} %bitcast.81, bf16[640,1024]{1,0:T(8,128)(2,1)S(1)} %bitcast.85), kind=kOutput, calls=%fused_computation | convolution fusion | flops 2020081664 | bytes 6750208 | tf_op jit(solution)/shard_map/dot_general | solution.py:14
  53.7 5.4 %all-to-all-start.1 = ((bf16[32,24,640]{2,1,0:T(8,128)(2,1)}), bf16[32,24,640]{2,1,0:T(8,128)(2,1)S(1)}, u32[]{:S(2)}, u32[]{:S(2)}) async-start(bf16[32,24,640]{2,1,0:T(8,128)(2,1)} %bitcast.5), calls=%async_computation.1 | async-start | bytes 1966080 | tf_op jit(solution)/shard_map/all_to_all | solution.py:106
  61.8 22.6 %all-to-all-done.1 = bf16[32,24,640]{2,1,0:T(8,128)(2,1)S(1)} async-done(((bf16[32,24,640]{2,1,0:T(8,128)(2,1)}), bf16[32,24,640]{2,1,0:T(8,128)(2,1)S(1)}, u32[]{:S(2)}, u32[]{:S(2)}) %all-to-all-start.1) | async-done | bytes 983072 | tf_op jit(solution)/shard_map/all_to_all | solution.py:106
  85.4 5.4 %all-to-all-start.2 = ((bf16[32,16,1280]{2,1,0:T(8,128)(2,1)}), bf16[32,16,1280]{2,1,0:T(8,128)(2,1)S(1)}, u32[]{:S(2)}, u32[]{:S(2)}) async-start(bf16[32,16,1280]{2,1,0:T(8,128)(2,1)} %pad_maximum_fusion.2), calls=%async_computation.3 | async-start | bytes 2621440 | tf_op jit(solution)/shard_map/all_to_all | solution.py:106
  94.6 2.9 collective-permute-start.2
  99.0 7.9 %collective-permute-done.2 = bf16[192,1024]{1,0:T(8,128)(2,1)S(1)} collective-permute-done((bf16[192,1024]{1,0:T(8,128)(2,1)}, bf16[192,1024]{1,0:T(8,128)(2,1)S(1)}, u32[]{:S(2)}, u32[]{:S(2)}) %collective-permute-start.2) | collective-permute-done | bytes 393248 | tf_op jit(solution)/shard_map/ppermute | solution.py:37
  106.9 8.8 %collective-permute-done.1 = bf16[192,1024]{1,0:T(8,128)(2,1)S(1)} collective-permute-done((bf16[192,1024]{1,0:T(8,128)(2,1)}, bf16[192,1024]{1,0:T(8,128)(2,1)S(1)}, u32[]{:S(2)}, u32[]{:S(2)}) %collective-permute-start.1) | collective-permute-done | bytes 393248 | tf_op jit(solution)/shard_map/ppermute | solution.py:37
  118.2 4.2 %collective-permute-start.3 = (bf16[192,1024]{1,0:T(8,128)(2,1)}, bf16[192,1024]{1,0:T(8,128)(2,1)}, u32[]{:S(2)}, u32[]{:S(2)}) collective-permute-start(bf16[192,1024]{1,0:T(8,128)(2,1)} %get-tuple-element.22), channel_id=1, source_target_pairs={{0,32},{32,0},{1,33},{33,1},{2,34},{34,2},{3,35},{35,3},{4,36},{36... | collective-permute-start | bytes 1179656 | tf_op jit(solution)/shard_map/ppermute | solution.py:41
  125.3 3.2 %convolution_convert_fusion.1 = bf16[512,2048]{1,0:T(8,128)(2,1)} fusion(bf16[512,1280]{1,0:T(8,128)(2,1)S(1)} %bitcast.65, bf16[640,1024]{1,0:T(8,128)(2,1)S(1)} %bitcast.82, bf16[640,1024]{1,0:T(8,128)(2,1)S(1)} %bitcast.86), kind=kOutput, calls=%fused_computation.4 | convolution fusion | flops 1348468736 | bytes 5373952 | tf_op jit(solution)/shard_map/dot_general | solution.py:14
  128.4 4.2 %collective-permute-start.4 = (bf16[192,2048]{1,0:T(8,128)(2,1)}, bf16[192,2048]{1,0:T(8,128)(2,1)S(1)}, u32[]{:S(2)}, u32[]{:S(2)}) collective-permute-start(bf16[192,2048]{1,0:T(8,128)(2,1)} %reduce-scatter.2.cloned.1.call-done), channel_id=1, source_target_pairs={{0,32},{32,0},{1,33},{33,1},{2,34},{34,2},{3,35},{35,3},{4,36},{36... | collective-permute-start | bytes 2359304 | tf_op jit(solution)/shard_map/ppermute | solution.py:41
  139.4 32.8 %collective-permute-done.4 = bf16[192,2048]{1,0:T(8,128)(2,1)S(1)} collective-permute-done((bf16[192,2048]{1,0:T(8,128)(2,1)}, bf16[192,2048]{1,0:T(8,128)(2,1)S(1)}, u32[]{:S(2)}, u32[]{:S(2)}) %collective-permute-start.4) | collective-permute-done | bytes 786464 | tf_op jit(solution)/shard_map/ppermute | solution.py:41
  178.5 8.8 %collective-permute-start.12 = (bf16[128,3072]{1,0:T(8,128)(2,1)}, bf16[128,3072]{1,0:T(8,128)(2,1)}, u32[]{:S(2)}, u32[]{:S(2)}) collective-permute-start(bf16[128,3072]{1,0:T(8,128)(2,1)} %fusion.35), channel_id=1, source_target_pairs={{0,32},{32,0},{1,33},{33,1},{2,34},{34,2},{3,35},{35,3},{4,36},{36... | collective-permute-start | bytes 2359304 | tf_op jit(solution)/shard_map/ppermute | solution.py:41
  188.0 14.0 %collective-permute-done.8 = bf16[192,3072]{1,0:T(8,128)(2,1)} collective-permute-done((bf16[192,3072]{1,0:T(8,128)(2,1)S(1)}, bf16[192,3072]{1,0:T(8,128)(2,1)}, u32[]{:S(2)}, u32[]{:S(2)}) %collective-permute-start.8) | collective-permute-done | bytes 1179680 | tf_op jit(solution)/shard_map/ppermute | solution.py:37
  204.3 2.7 collective-permute-start.11
  214.0 3.1 %collective-permute-done.10 = bf16[96,3072]{1,0:T(8,128)(2,1)S(1)} collective-permute-done((bf16[96,3072]{1,0:T(8,128)(2,1)S(1)}, bf16[96,3072]{1,0:T(8,128)(2,1)S(1)}, u32[]{:S(2)}, u32[]{:S(2)}) %collective-permute-start.10) | collective-permute-done | bytes 589856 | tf_op jit(solution)/shard_map/ppermute | solution.py:37
  220.8 3.6 %fusion.9 = bf16[768,640]{1,0:T(8,128)(2,1)} fusion(bf16[768,3072]{1,0:T(8,128)(2,1)S(1)} %constant_dynamic-update-slice_fusion.5, bf16[640,1024]{1,0:T(8,128)(2,1)S(1)} %bitcast.83, bf16[640,1024]{1,0:T(8,128)(2,1)S(1)} %bitcast.87), kind=kOutput, calls=%fused_computation.23 | convolution fusion | flops 2019000320 | bytes 6750208 | tf_op jit(solution)/shard_map/dot_general | solution.py:14
  224.4 15.6 %all-to-all-start.3 = ((bf16[32,24,640]{2,1,0:T(8,128)(2,1)}), bf16[32,24,640]{2,1,0:T(8,128)(2,1)}, u32[]{:S(2)}, u32[]{:S(2)}) async-start(bf16[32,24,640]{2,1,0:T(8,128)(2,1)} %bitcast.17), calls=%async_computation.4 | async-start | bytes 1966080 | tf_op jit(solution)/shard_map/all_to_all | solution.py:106
  250.5 2.7 fusion.5
  256.9 2.7 fusion.17
  259.6 5.8 %all-to-all-done.3 = bf16[32,24,640]{2,1,0:T(8,128)(2,1)} async-done(((bf16[32,24,640]{2,1,0:T(8,128)(2,1)}), bf16[32,24,640]{2,1,0:T(8,128)(2,1)}, u32[]{:S(2)}, u32[]{:S(2)}) %all-to-all-start.3) | async-done | bytes 983072 | tf_op jit(solution)/shard_map/all_to_all | solution.py:106
  265.4 6.0 %all-to-all-start.4 = ((bf16[32,16,640]{2,1,0:T(8,128)(2,1)}), bf16[32,16,640]{2,1,0:T(8,128)(2,1)}, u32[]{:S(2)}, u32[]{:S(2)}) async-start(bf16[32,16,640]{2,1,0:T(8,128)(2,1)} %bitcast.77), calls=%async_computation.5 | async-start | bytes 1310720 | tf_op jit(solution)/shard_map/all_to_all | solution.py:106
  275.7 3.8 %fusion.12 = bf16[1,640,1024]{2,1,0:T(8,128)(2,1)} fusion(f32[640,1024]{1,0:T(8,128)S(1)} %fusion.25, bf16[768,640]{1,0:T(8,128)(2,1)S(1)} %bitcast.73, bf16[768,3072]{1,0:T(8,128)(2,1)} %copy-done.5), kind=kOutput, calls=%fused_computation.24 | convolution fusion | flops 1007943680 | bytes 6488064 | tf_op jit(solution)/shard_map/dot_general | solution.py:14
  281.1 9.2 %all-to-all-done.4 = bf16[32,16,640]{2,1,0:T(8,128)(2,1)} async-done(((bf16[32,16,640]{2,1,0:T(8,128)(2,1)}), bf16[32,16,640]{2,1,0:T(8,128)(2,1)}, u32[]{:S(2)}, u32[]{:S(2)}) %all-to-all-start.4) | async-done | bytes 655392 | tf_op jit(solution)/shard_map/all_to_all | solution.py:106
  (158 shorter events, 70.0 us)
Async XLA Ops:
  7.2 83.7 %copy-start = (bf16[1,640,1024]{2,1,0:T(8,128)(2,1)S(1)}, bf16[1,640,1024]{2,1,0:T(8,128)(2,1)}, u32[]{:S(2)}) copy-start(bf16[1,640,1024]{2,1,0:T(8,128)(2,1)} %param.15) | copy-start | bytes 3932164
  7.2 121.2 %reduce-scatter.2.cloned.1.call-start = ((), (), s32[]{:S(2)}) async-start(), calls=%async_computation.6 | async-start | bytes 3932160 | tf_op jit(solution)/shard_map/reduce_scatter | solution.py:60
  8.3 38.9 %copy-start.32 = (bf16[1,640,1024]{2,1,0:T(8,128)(2,1)S(1)}, bf16[1,640,1024]{2,1,0:T(8,128)(2,1)}, u32[]{:S(2)}) copy-start(bf16[1,640,1024]{2,1,0:T(8,128)(2,1)} %param.13) | copy-start | bytes 3932164
  53.7 30.7 %all-to-all-start.1 = ((bf16[32,24,640]{2,1,0:T(8,128)(2,1)}), bf16[32,24,640]{2,1,0:T(8,128)(2,1)S(1)}, u32[]{:S(2)}, u32[]{:S(2)}) async-start(bf16[32,24,640]{2,1,0:T(8,128)(2,1)} %bitcast.5), calls=%async_computation.1 | async-start | bytes 1966080 | tf_op jit(solution)/shard_map/all_to_all | solution.py:106
  85.4 37.3 %all-to-all-start.2 = ((bf16[32,16,1280]{2,1,0:T(8,128)(2,1)}), bf16[32,16,1280]{2,1,0:T(8,128)(2,1)S(1)}, u32[]{:S(2)}, u32[]{:S(2)}) async-start(bf16[32,16,1280]{2,1,0:T(8,128)(2,1)} %pad_maximum_fusion.2), calls=%async_computation.3 | async-start | bytes 2621440 | tf_op jit(solution)/shard_map/all_to_all | solution.py:106
  94.6 12.3 %collective-permute-start.2 = (bf16[192,1024]{1,0:T(8,128)(2,1)}, bf16[192,1024]{1,0:T(8,128)(2,1)S(1)}, u32[]{:S(2)}, u32[]{:S(2)}) collective-permute-start(bf16[192,1024]{1,0:T(8,128)(2,1)} %get-tuple-element.35), channel_id=1, source_target_pairs={{0,128},{64,192},{128,0},{192,64},{1,129},{65,193},{129,1},{193,65... | collective-permute-start | bytes 1179656 | tf_op jit(solution)/shard_map/ppermute | solution.py:37
  97.5 18.2 %collective-permute-start.1 = (bf16[192,1024]{1,0:T(8,128)(2,1)}, bf16[192,1024]{1,0:T(8,128)(2,1)S(1)}, u32[]{:S(2)}, u32[]{:S(2)}) collective-permute-start(bf16[192,1024]{1,0:T(8,128)(2,1)} %get-tuple-element.36), channel_id=1, source_target_pairs={{0,192},{64,0},{128,64},{192,128},{1,193},{65,1},{129,65},{193,129... | collective-permute-start | bytes 1179656 | tf_op jit(solution)/shard_map/ppermute | solution.py:37
  98.3 17.6 %collective-permute-start = (bf16[192,1024]{1,0:T(8,128)(2,1)}, bf16[192,1024]{1,0:T(8,128)(2,1)}, u32[]{:S(2)}, u32[]{:S(2)}) collective-permute-start(bf16[192,1024]{1,0:T(8,128)(2,1)} %get-tuple-element.34), channel_id=1, source_target_pairs={{0,64},{64,128},{128,192},{192,0},{1,65},{65,129},{129,193},{193,1... | collective-permute-start | bytes 1179656 | tf_op jit(solution)/shard_map/ppermute | solution.py:37
  118.2 54.1 %collective-permute-start.3 = (bf16[192,1024]{1,0:T(8,128)(2,1)}, bf16[192,1024]{1,0:T(8,128)(2,1)}, u32[]{:S(2)}, u32[]{:S(2)}) collective-permute-start(bf16[192,1024]{1,0:T(8,128)(2,1)} %get-tuple-element.22), channel_id=1, source_target_pairs={{0,32},{32,0},{1,33},{33,1},{2,34},{34,2},{3,35},{35,3},{4,36},{36... | collective-permute-start | bytes 1179656 | tf_op jit(solution)/shard_map/ppermute | solution.py:41
  128.4 43.7 %collective-permute-start.4 = (bf16[192,2048]{1,0:T(8,128)(2,1)}, bf16[192,2048]{1,0:T(8,128)(2,1)S(1)}, u32[]{:S(2)}, u32[]{:S(2)}) collective-permute-start(bf16[192,2048]{1,0:T(8,128)(2,1)} %reduce-scatter.2.cloned.1.call-done), channel_id=1, source_target_pairs={{0,32},{32,0},{1,33},{33,1},{2,34},{34,2},{3,35},{35,3},{4,36},{36... | collective-permute-start | bytes 2359304 | tf_op jit(solution)/shard_map/ppermute | solution.py:41
  134.7 39.6 %collective-permute-start.5 = (bf16[128,3072]{1,0:T(8,128)(2,1)S(1)}, bf16[128,3072]{1,0:T(8,128)(2,1)S(1)}, u32[]{:S(2)}, u32[]{:S(2)}) collective-permute-start(bf16[128,3072]{1,0:T(8,128)(2,1)S(1)} %get-tuple-element.28), channel_id=1, source_target_pairs={{0,64},{64,128},{128,192},{192,0},{1,65},{65,129},{129,193},{193,1... | collective-permute-start | bytes 2359304 | tf_op jit(solution)/shard_map/ppermute | solution.py:37
  136.3 38.0 %collective-permute-start.6 = (bf16[128,3072]{1,0:T(8,128)(2,1)S(1)}, bf16[128,3072]{1,0:T(8,128)(2,1)S(1)}, u32[]{:S(2)}, u32[]{:S(2)}) collective-permute-start(bf16[128,3072]{1,0:T(8,128)(2,1)S(1)} %get-tuple-element.27), channel_id=1, source_target_pairs={{0,192},{64,0},{128,64},{192,128},{1,193},{65,1},{129,65},{193,129... | collective-permute-start | bytes 2359304 | tf_op jit(solution)/shard_map/ppermute | solution.py:37
  137.8 36.5 %collective-permute-start.7 = (bf16[128,3072]{1,0:T(8,128)(2,1)S(1)}, bf16[128,3072]{1,0:T(8,128)(2,1)S(1)}, u32[]{:S(2)}, u32[]{:S(2)}) collective-permute-start(bf16[128,3072]{1,0:T(8,128)(2,1)S(1)} %get-tuple-element.26), channel_id=1, source_target_pairs={{0,128},{64,192},{128,0},{192,64},{1,129},{65,193},{129,1},{193,65... | collective-permute-start | bytes 2359304 | tf_op jit(solution)/shard_map/ppermute | solution.py:37
  174.3 27.7 %collective-permute-start.8 = (bf16[192,3072]{1,0:T(8,128)(2,1)S(1)}, bf16[192,3072]{1,0:T(8,128)(2,1)}, u32[]{:S(2)}, u32[]{:S(2)}) collective-permute-start(bf16[192,3072]{1,0:T(8,128)(2,1)S(1)} %pad_maximum_fusion.3), channel_id=1, source_target_pairs={{0,64},{64,128},{128,192},{192,0},{1,65},{65,129},{129,193},{193,1... | collective-permute-start | bytes 3538952 | tf_op jit(solution)/shard_map/ppermute | solution.py:37
  174.5 28.7 %collective-permute-start.9 = (bf16[192,3072]{1,0:T(8,128)(2,1)S(1)}, bf16[192,3072]{1,0:T(8,128)(2,1)}, u32[]{:S(2)}, u32[]{:S(2)}) collective-permute-start(bf16[192,3072]{1,0:T(8,128)(2,1)S(1)} %pad_maximum_fusion.3), channel_id=1, source_target_pairs={{0,192},{64,0},{128,64},{192,128},{1,193},{65,1},{129,65},{193,129... | collective-permute-start | bytes 3538952 | tf_op jit(solution)/shard_map/ppermute | solution.py:37
  178.5 29.5 %collective-permute-start.12 = (bf16[128,3072]{1,0:T(8,128)(2,1)}, bf16[128,3072]{1,0:T(8,128)(2,1)}, u32[]{:S(2)}, u32[]{:S(2)}) collective-permute-start(bf16[128,3072]{1,0:T(8,128)(2,1)} %fusion.35), channel_id=1, source_target_pairs={{0,32},{32,0},{1,33},{33,1},{2,34},{34,2},{3,35},{35,3},{4,36},{36... | collective-permute-start | bytes 2359304 | tf_op jit(solution)/shard_map/ppermute | solution.py:41
  203.1 14.0 %collective-permute-start.10 = (bf16[96,3072]{1,0:T(8,128)(2,1)S(1)}, bf16[96,3072]{1,0:T(8,128)(2,1)S(1)}, u32[]{:S(2)}, u32[]{:S(2)}) collective-permute-start(bf16[96,3072]{1,0:T(8,128)(2,1)S(1)} %slice.83), channel_id=1, source_target_pairs={{0,64},{64,128},{128,192},{192,0},{1,65},{65,129},{129,193},{193,1... | collective-permute-start | bytes 1769480 | tf_op jit(solution)/shard_map/ppermute | solution.py:37
  204.3 13.0 %collective-permute-start.11 = (bf16[96,3072]{1,0:T(8,128)(2,1)S(1)}, bf16[96,3072]{1,0:T(8,128)(2,1)S(1)}, u32[]{:S(2)}, u32[]{:S(2)}) collective-permute-start(bf16[96,3072]{1,0:T(8,128)(2,1)S(1)} %slice.84), channel_id=1, source_target_pairs={{0,192},{64,0},{128,64},{192,128},{1,193},{65,1},{129,65},{193,129... | collective-permute-start | bytes 1769480 | tf_op jit(solution)/shard_map/ppermute | solution.py:37
  217.3 24.5 %collective-permute-start.13 = (bf16[128,3072]{1,0:T(8,128)(2,1)}, bf16[128,3072]{1,0:T(8,128)(2,1)}, u32[]{:S(2)}, u32[]{:S(2)}) collective-permute-start(bf16[128,3072]{1,0:T(8,128)(2,1)} %pad_maximum_fusion.4), channel_id=1, source_target_pairs={{0,64},{64,128},{128,192},{192,0},{1,65},{65,129},{129,193},{193,1... | collective-permute-start | bytes 2359304 | tf_op jit(solution)/shard_map/ppermute | solution.py:37
  218.3 24.7 %collective-permute-start.14 = (bf16[128,3072]{1,0:T(8,128)(2,1)}, bf16[128,3072]{1,0:T(8,128)(2,1)}, u32[]{:S(2)}, u32[]{:S(2)}) collective-permute-start(bf16[128,3072]{1,0:T(8,128)(2,1)} %pad_maximum_fusion.4), channel_id=1, source_target_pairs={{0,192},{64,0},{128,64},{192,128},{1,193},{65,1},{129,65},{193,129... | collective-permute-start | bytes 2359304 | tf_op jit(solution)/shard_map/ppermute | solution.py:37
  224.4 41.0 %all-to-all-start.3 = ((bf16[32,24,640]{2,1,0:T(8,128)(2,1)}), bf16[32,24,640]{2,1,0:T(8,128)(2,1)}, u32[]{:S(2)}, u32[]{:S(2)}) async-start(bf16[32,24,640]{2,1,0:T(8,128)(2,1)} %bitcast.17), calls=%async_computation.4 | async-start | bytes 1966080 | tf_op jit(solution)/shard_map/all_to_all | solution.py:106
  242.9 11.8 %collective-permute-start.15 = (bf16[64,3072]{1,0:T(8,128)(2,1)S(1)}, bf16[64,3072]{1,0:T(8,128)(2,1)S(1)}, u32[]{:S(2)}, u32[]{:S(2)}) collective-permute-start(bf16[64,3072]{1,0:T(8,128)(2,1)S(1)} %slice.89), channel_id=1, source_target_pairs={{0,64},{64,128},{128,192},{192,0},{1,65},{65,129},{129,193},{193,1... | collective-permute-start | bytes 1179656 | tf_op jit(solution)/shard_map/ppermute | solution.py:37
  244.3 10.6 %collective-permute-start.16 = (bf16[64,3072]{1,0:T(8,128)(2,1)S(1)}, bf16[64,3072]{1,0:T(8,128)(2,1)S(1)}, u32[]{:S(2)}, u32[]{:S(2)}) collective-permute-start(bf16[64,3072]{1,0:T(8,128)(2,1)S(1)} %slice.90), channel_id=1, source_target_pairs={{0,192},{64,0},{128,64},{192,128},{1,193},{65,1},{129,65},{193,129... | collective-permute-start | bytes 1179656 | tf_op jit(solution)/shard_map/ppermute | solution.py:37
  265.4 25.0 %all-to-all-start.4 = ((bf16[32,16,640]{2,1,0:T(8,128)(2,1)}), bf16[32,16,640]{2,1,0:T(8,128)(2,1)}, u32[]{:S(2)}, u32[]{:S(2)}) async-start(bf16[32,16,640]{2,1,0:T(8,128)(2,1)} %bitcast.77), calls=%async_computation.5 | async-start | bytes 1310720 | tf_op jit(solution)/shard_map/all_to_all | solution.py:106
  (34 other events, 362.6 us)
Sparse Core Ops, SparseCore 0:
  51.5 39.9 reduce-scatter.1
